TPU v7x, 256 devices: a whole 4x4x8 slice. The times are simulated.
256 devices in a mesh: dom: 8 (over y, core), dev: 32 (over z, x).
Axes of the slice: x: 4, y: 4, z: 8, core: 2. Of those that a mesh axis runs over, the one named last changes fastest.
Arguments:
- start_block: float32 [589824, 128], P(('dom', 'dev')), may hold values from -8 to 8
- columns: int32 [4608, 4], P(('dom', 'dev')), may hold values from 0 to 4607, as said below
- edge_weights: int32 [4608, 4, 128, 128], P(('dom', 'dev')), may hold values from 0 to 1023, as said below
Outputs:
- filtered: float32 [589824, 128], P(('dom', 'dev'))
- ritz: float32 [128, 128], replicated
Inputs may be any that keep to these rules, and one draw needn't show every extreme that they name: `columns`: A device holds 18 consecutive tile-rows, and a part 32 consecutive devices. Each tile-row lists first its own diagonal tile, then a tile of the same device. Over one device's tile-rows, exactly one reference goes to each device of the same part whose index within the part differs from its own by 1 to 4, cyclically, in either direction, and exactly one to the device of the same part whose index differs by 16; 8 references go to the device of the same index within another part, every other part once and one of them twice; all other references are to tiles of the same device. `edge_weights`: each row of a tile-row has its own power of two between 16 and 1024 that bounds its entries; the diagonal entries of the diagonal tile are at least half of that power.
All inputs are finite; a program needn't handle non-finite values.
Results may differ from a plain program's by a relative error of at most 0.0003.
Values sent between devices are 32-bit elements; how exact they have to be, the bound alone decides.
A program may use at most 128 MiB of HBM per device.

v0:
```python
import jax
import jax.numpy as jnp
from jax import lax
from jax.sharding import PartitionSpec as P

DEGREE = 5
CAPX = 2


epsilon = 1e-06
center = 1.025
half_width = 0.975


def body(start_block, columns, edge_weights):
    tile_rows = columns.shape[0]
    tile_size = edge_weights.shape[2]
    width = start_block.shape[1]
    dev_count = lax.axis_size("dev")
    dom_count = lax.axis_size("dom")
    dev_index = lax.axis_index("dev")
    dom_index = lax.axis_index("dom")
    own_device = dom_index * dev_count + dev_index
    total_rows = tile_rows * tile_size * dev_count * dom_count
    weights_float = edge_weights.astype(jnp.float32)
    degree = jnp.sum(weights_float, axis=(1, 3))
    row_scale = lax.rsqrt(degree)
    owner = columns // tile_rows
    local_tile = columns % tile_rows
    owner_part = owner // dev_count
    owner_dev = owner % dev_count
    is_local = owner == own_device
    is_inner = (owner_part == dom_index) & jnp.logical_not(is_local)
    is_outer = owner_part != dom_index
    flat_outer = is_outer.reshape(-1)
    flat_part = owner_part.reshape(-1)
    entry_ids = jnp.arange(flat_outer.shape[0], dtype=jnp.int32)
    same_group = (
        flat_outer[:, None] & flat_outer[None, :] & (flat_part[:, None] == flat_part[None, :])
    )
    earlier = entry_ids[None, :] < entry_ids[:, None]
    ranks = jnp.sum((same_group & earlier).astype(jnp.int32), axis=1).reshape(columns.shape)
    outer_slot = owner_part * CAPX + ranks
    source_index = jnp.where(
        is_local,
        local_tile,
        jnp.where(is_inner, tile_rows + owner_dev, tile_rows + dev_count + outer_slot),
    )
    peer_ids = jnp.arange(dev_count, dtype=jnp.int32)
    wanted_inner = jnp.sum(
        jnp.where(
            is_inner.reshape(-1)[None, :] & (owner_dev.reshape(-1)[None, :] == peer_ids[:, None]),
            local_tile.reshape(-1)[None, :],
            0,
        ),
        axis=1,
    )
    slot_ids = jnp.arange(dom_count * CAPX, dtype=jnp.int32)
    wanted_outer = jnp.sum(
        jnp.where(
            flat_outer[None, :] & (outer_slot.reshape(-1)[None, :] == slot_ids[:, None]),
            local_tile.reshape(-1)[None, :],
            0,
        ),
        axis=1,
    )
    serve_inner = lax.all_to_all(wanted_inner, "dev", split_axis=0, concat_axis=0, tiled=True)
    serve_outer = lax.all_to_all(wanted_outer, "dom", split_axis=0, concat_axis=0, tiled=True)

    def apply_laplacian(field):
        scaled = row_scale[:, :, None] * field
        inner = lax.all_to_all(scaled[serve_inner], "dev", split_axis=0, concat_axis=0, tiled=True)
        outer = lax.all_to_all(scaled[serve_outer], "dom", split_axis=0, concat_axis=0, tiled=True)
        sources = jnp.concatenate([scaled, inner, outer], axis=0)
        operand = sources[source_index]
        product = jnp.einsum(
            "rkij,rkjw->riw",
            weights_float,
            operand,
            precision=lax.Precision.HIGHEST,
            preferred_element_type=jnp.float32,
        )
        return field - row_scale[:, :, None] * product

    field = start_block.reshape(tile_rows, tile_size, width)
    squares = jnp.sum(field * field, axis=(0, 1))
    totals = lax.psum(squares, ("dom", "dev"))
    factor = lax.rsqrt(totals / total_rows + epsilon)
    first = field * factor
    older = first
    newer = (apply_laplacian(first) - center * first) / half_width
    for degree_step in range(2, DEGREE + 1):
        older, newer = (newer, 2.0 * (apply_laplacian(newer) - center * newer) / half_width - older)
    field = newer
    flat = field.reshape(tile_rows * tile_size, width)
    basis_part = jnp.dot(
        flat.T, flat, precision=lax.Precision.HIGHEST, preferred_element_type=jnp.float32
    )
    image = apply_laplacian(field)
    ritz_part = jnp.dot(
        flat.T,
        image.reshape(tile_rows * tile_size, width),
        precision=lax.Precision.HIGHEST,
        preferred_element_type=jnp.float32,
    )
    gram, projected = lax.psum((basis_part, ritz_part), ("dom", "dev"))
    gram = gram / total_rows
    projected = projected / total_rows
    lower = jnp.linalg.cholesky(gram)
    left_solved = jax.scipy.linalg.solve_triangular(lower, projected, lower=True)
    ritz = jax.scipy.linalg.solve_triangular(lower, left_solved.T, lower=True).T
    return (flat, ritz)


def solution(mesh):
    in_specs = (
        P(("dom", "dev"), None),
        P(("dom", "dev"), None),
        P(("dom", "dev"), None, None, None),
    )
    out_specs = (P(("dom", "dev"), None), P())
    return jax.shard_map(body, mesh=mesh, in_specs=in_specs, out_specs=out_specs, check_vma=False)
```

profile of v0, /device:TPU:1, one launch (start us, length us, event | category | flops | bytes accessed | tf_op | source)
XLA Modules:
  0.0 960.9 jit_solution(12299866124629234046)
XLA Ops:
  9.5 6.5 all-to-all-start.2
  17.5 80.0 %psum.21 = f32[128]{0:T(128)S(1)} all-reduce(f32[128]{0:T(128)S(1)} %multiply_reduce_fusion), channel_id=1, replica_groups=mesh['dom'=8,'dev'=32] {'dom','dev'}, use_global_device_ids=true, to_apply=%region_1.2 | all-reduce | flops 128 | bytes 1024 | tf_op jit(solution)/shard_map/psum | solution.py:87
  102.3 5.4 all-to-all-start
  110.6 5.6 all-to-all-done
  116.2 5.6 all-to-all-start.3
  124.5 12.4 %all-to-all-done.3 = f32[16,128,128]{2,1,0:T(8,128)S(1)} async-done(((f32[16,128,128]{2,1,0:T(8,128)}), f32[16,128,128]{2,1,0:T(8,128)S(1)}, u32[]{:S(2)}, u32[]{:S(2)}) %all-to-all-start.3) | async-done | bytes 1048608 | tf_op jit(solution)/shard_map/all_to_all | solution.py:73
  141.8 48.3 %all-to-all-done.1 = f32[32,128,128]{2,1,0:T(8,128)} async-done(((f32[32,128,128]{2,1,0:T(8,128)}), f32[32,128,128]{2,1,0:T(8,128)}, u32[]{:S(2)}, u32[]{:S(2)}) %all-to-all-start.1) | async-done | bytes 2097184 | tf_op jit(solution)/shard_map/all_to_all | solution.py:72
  199.3 9.0 broadcast_multiply_fusion
  210.0 7.5 all-to-all-start.5
  219.6 13.1 %all-to-all-done.5 = f32[16,128,128]{2,1,0:T(8,128)} async-done(((f32[16,128,128]{2,1,0:T(8,128)}), f32[16,128,128]{2,1,0:T(8,128)}, u32[]{:S(2)}, u32[]{:S(2)}) %all-to-all-start.5) | async-done | bytes 1048608 | tf_op jit(solution)/shard_map/all_to_all | solution.py:73
  232.7 54.0 %all_to_all.84 = f32[32,128,128]{2,1,0:T(8,128)S(1)} all-to-all(f32[32,128,128]{2,1,0:T(8,128)} %gather_fusion.3), channel_id=1, replica_groups=mesh['dom'=8,'dev'=32] {'dev'}, dimensions={0} | all-to-all | bytes 4194304 | tf_op jit(solution)/shard_map/all_to_all | solution.py:72
  295.7 10.0 %broadcast_multiply_fusion.4 = (f32[18,128,128]{2,1,0:T(8,128)S(1)}, f32[18,128,128]{2,1,0:T(8,128)}) fusion(f32[18,128]{1,0:T(8,128)S(1)} %get-tuple-element.21, f32[18,128,128]{2,1,0:T(8,128)S(1)} %bitcast.176, f32[128]{0:T(128)} %copy-done.6, f32[18,128,128]{2,1,0:T(8,128)S(1)} %get-tuple-element.25, f32[18,4,128,128]{3,2,1,0:T(8,128)} %bitcast.177, ...), kind=kOutput, calls=%fused_computation.85 | convolution fusion | flops 1815773184 | bytes 14165504 | tf_op jit(solution)/shard_map/rkij,rkjw->riw/dot_general | solution.py:76
  307.4 6.4 all-to-all-start.7
  316.0 13.0 %all-to-all-done.7 = f32[16,128,128]{2,1,0:T(8,128)S(1)} async-done(((f32[16,128,128]{2,1,0:T(8,128)}), f32[16,128,128]{2,1,0:T(8,128)S(1)}, u32[]{:S(2)}, u32[]{:S(2)}) %all-to-all-start.7) | async-done | bytes 1048608 | tf_op jit(solution)/shard_map/all_to_all | solution.py:73
  328.9 54.0 %all_to_all.85 = f32[32,128,128]{2,1,0:T(8,128)S(1)} all-to-all(f32[32,128,128]{2,1,0:T(8,128)} %gather_fusion.6), channel_id=1, replica_groups=mesh['dom'=8,'dev'=32] {'dev'}, dimensions={0} | all-to-all | bytes 4194304 | tf_op jit(solution)/shard_map/all_to_all | solution.py:72
  390.7 10.0 %broadcast_multiply_fusion.3 = (f32[18,128,128]{2,1,0:T(8,128)S(1)}, f32[18,128,128]{2,1,0:T(8,128)}) fusion(f32[18,128]{1,0:T(8,128)S(1)} %get-tuple-element.21, f32[18,128,128]{2,1,0:T(8,128)S(1)} %get-tuple-element.25, f32[18,128,128]{2,1,0:T(8,128)S(1)} %copy-done.2, f32[18,4,128,128]{3,2,1,0:T(8,128)} %bitcast.180, s32[18,4,128,128]{3,2,1,0:T(8,128)} %param.7), kind=kOutput, calls=%fused_computation.84 | convolution fusion | flops 1815478272 | bytes 14164992 | tf_op jit(solution)/shard_map/rkij,rkjw->riw/dot_general | solution.py:76
  402.3 6.4 all-to-all-start.9
  410.9 13.0 %all-to-all-done.9 = f32[16,128,128]{2,1,0:T(8,128)S(1)} async-done(((f32[16,128,128]{2,1,0:T(8,128)}), f32[16,128,128]{2,1,0:T(8,128)S(1)}, u32[]{:S(2)}, u32[]{:S(2)}) %all-to-all-start.9) | async-done | bytes 1048608 | tf_op jit(solution)/shard_map/all_to_all | solution.py:73
  423.9 54.0 %all_to_all.86 = f32[32,128,128]{2,1,0:T(8,128)S(1)} all-to-all(f32[32,128,128]{2,1,0:T(8,128)} %gather_fusion.9), channel_id=1, replica_groups=mesh['dom'=8,'dev'=32] {'dev'}, dimensions={0} | all-to-all | bytes 4194304 | tf_op jit(solution)/shard_map/all_to_all | solution.py:72
  485.7 10.0 %broadcast_multiply_fusion.2 = (f32[18,128,128]{2,1,0:T(8,128)S(1)}, f32[18,128,128]{2,1,0:T(8,128)}) fusion(f32[18,128]{1,0:T(8,128)S(1)} %get-tuple-element.21, f32[18,128,128]{2,1,0:T(8,128)S(1)} %copy-done.2, f32[18,128,128]{2,1,0:T(8,128)S(1)} %copy-done.3, f32[18,4,128,128]{3,2,1,0:T(8,128)} %bitcast.181, s32[18,4,128,128]{3,2,1,0:T(8,128)} %param.7), kind=kOutput, calls=%fused_computation.83 | convolution fusion | flops 1815183360 | bytes 14164992 | tf_op jit(solution)/shard_map/rkij,rkjw->riw/dot_general | solution.py:76
  497.4 6.4 all-to-all-start.11
  506.0 13.0 %all-to-all-done.11 = f32[16,128,128]{2,1,0:T(8,128)S(1)} async-done(((f32[16,128,128]{2,1,0:T(8,128)}), f32[16,128,128]{2,1,0:T(8,128)S(1)}, u32[]{:S(2)}, u32[]{:S(2)}) %all-to-all-start.11) | async-done | bytes 1048608 | tf_op jit(solution)/shard_map/all_to_all | solution.py:73
  518.9 54.0 %all_to_all.87 = f32[32,128,128]{2,1,0:T(8,128)S(1)} all-to-all(f32[32,128,128]{2,1,0:T(8,128)} %gather_fusion.12), channel_id=1, replica_groups=mesh['dom'=8,'dev'=32] {'dev'}, dimensions={0} | all-to-all | bytes 4194304 | tf_op jit(solution)/shard_map/all_to_all | solution.py:72
  580.6 9.2 broadcast_multiply_fusion.1
  591.6 6.4 all-to-all-start.13
  600.1 13.0 %all-to-all-done.13 = f32[16,128,128]{2,1,0:T(8,128)S(1)} async-done(((f32[16,128,128]{2,1,0:T(8,128)}), f32[16,128,128]{2,1,0:T(8,128)S(1)}, u32[]{:S(2)}, u32[]{:S(2)}) %all-to-all-start.13) | async-done | bytes 1048608 | tf_op jit(solution)/shard_map/all_to_all | solution.py:73
  613.1 5.4 all-to-all-start.12
  621.7 45.1 %all-to-all-done.12 = f32[32,128,128]{2,1,0:T(8,128)} async-done(((f32[32,128,128]{2,1,0:T(8,128)}), f32[32,128,128]{2,1,0:T(8,128)}, u32[]{:S(2)}, u32[]{:S(2)}) %all-to-all-start.12) | async-done | bytes 2097184 | tf_op jit(solution)/shard_map/all_to_all | solution.py:72
  676.2 9.2 fusion.35
  688.1 238.8 %all-reduce.3.cloned.1.call-done = (f32[128,128]{0,1:T(8,128)}, f32[128,128]{0,1:T(8,128)}) async-done(((f32[128,128]{0,1:T(8,128)}, f32[128,128]{0,1:T(8,128)}), (f32[128,128]{0,1:T(8,128)}, f32[128,128]{0,1:T(8,128)})) %all-reduce.3.cloned.1.call-update) | async-done | bytes 131088 | tf_op jit(solution)/shard_map/psum | solution.py:106
  928.7 11.9 %cholesky.18 = f32[128,128]{1,0:T(8,128)S(1)} custom-call(f32[128,128]{1,0:T(8,128)S(1)} %fusion.128), custom_call_target="Cholesky" | custom-call | tf_op jit(solution)/shard_map/jit(cholesky)/cholesky | solution.py:109
  941.9 9.8 %custom-call.8 = f32[1,128,128]{1,2,0:T(8,128)S(1)} custom-call(f32[1,128,128]{2,1,0:T(8,128)S(1)} %fusion.125), custom_call_target="InvertDiagBlocksLowerTriangular" | custom-call | tf_op jit(solution)/shard_map/jit(_solve_triangular)/triangular_solve | solution.py:111
  (83 shorter events, 100.3 us)
Async XLA Ops:
  9.5 92.8 %all-to-all-start.2 = ((s32[8,2,1]{1,2,0:T(1,128)}), s32[8,2,1]{1,2,0:T(1,128)S(1)}, u32[]{:S(2)}, u32[]{:S(2)}) async-start(s32[8,2,1]{1,2,0:T(1,128)} %bitcast.3), calls=%async_computation.2 | async-start | bytes 8192 | tf_op jit(solution)/shard_map/all_to_all | solution.py:68
  97.5 3.7 copy-start.6
  97.5 3.8 copy-start.1
  102.3 13.9 %all-to-all-start = ((s32[32,1,1]{2,1,0:T(1,128)}), s32[32,1,1]{2,1,0:T(1,128)S(1)}, u32[]{:S(2)}, u32[]{:S(2)}) async-start(s32[32,1,1]{2,1,0:T(1,128)} %copy.48), calls=%async_computation | async-start | bytes 32768 | tf_op jit(solution)/shard_map/all_to_all | solution.py:67
  109.0 7.2 copy-start.4
  116.2 20.7 %all-to-all-start.3 = ((f32[16,128,128]{2,1,0:T(8,128)}), f32[16,128,128]{2,1,0:T(8,128)S(1)}, u32[]{:S(2)}, u32[]{:S(2)}) async-start(f32[16,128,128]{2,1,0:T(8,128)} %gather_fusion.1), calls=%async_computation.3 | async-start | bytes 2097152 | tf_op jit(solution)/shard_map/all_to_all | solution.py:73
  122.5 2.0 copy-start.5
  136.9 53.1 %all-to-all-start.1 = ((f32[32,128,128]{2,1,0:T(8,128)}), f32[32,128,128]{2,1,0:T(8,128)}, u32[]{:S(2)}, u32[]{:S(2)}) async-start(f32[32,128,128]{2,1,0:T(8,128)} %gather_fusion), calls=%async_computation.1 | async-start | bytes 4194304 | tf_op jit(solution)/shard_map/all_to_all | solution.py:72
  210.0 22.7 %all-to-all-start.5 = ((f32[16,128,128]{2,1,0:T(8,128)}), f32[16,128,128]{2,1,0:T(8,128)}, u32[]{:S(2)}, u32[]{:S(2)}) async-start(f32[16,128,128]{2,1,0:T(8,128)} %gather_fusion.4), calls=%async_computation.5 | async-start | bytes 2097152 | tf_op jit(solution)/shard_map/all_to_all | solution.py:73
  307.4 21.6 %all-to-all-start.7 = ((f32[16,128,128]{2,1,0:T(8,128)}), f32[16,128,128]{2,1,0:T(8,128)S(1)}, u32[]{:S(2)}, u32[]{:S(2)}) async-start(f32[16,128,128]{2,1,0:T(8,128)} %gather_fusion.7), calls=%async_computation.7 | async-start | bytes 2097152 | tf_op jit(solution)/shard_map/all_to_all | solution.py:73
  385.3 5.3 copy-start.2
  402.3 21.6 %all-to-all-start.9 = ((f32[16,128,128]{2,1,0:T(8,128)}), f32[16,128,128]{2,1,0:T(8,128)S(1)}, u32[]{:S(2)}, u32[]{:S(2)}) async-start(f32[16,128,128]{2,1,0:T(8,128)} %gather_fusion.10), calls=%async_computation.9 | async-start | bytes 2097152 | tf_op jit(solution)/shard_map/all_to_all | solution.py:73
  480.4 5.3 copy-start.3
  497.4 21.6 %all-to-all-start.11 = ((f32[16,128,128]{2,1,0:T(8,128)}), f32[16,128,128]{2,1,0:T(8,128)S(1)}, u32[]{:S(2)}, u32[]{:S(2)}) async-start(f32[16,128,128]{2,1,0:T(8,128)} %gather_fusion.13), calls=%async_computation.11 | async-start | bytes 2097152 | tf_op jit(solution)/shard_map/all_to_all | solution.py:73
  589.9 95.5 %copy-start = (f32[18,128,128]{2,1,0:T(8,128)}, f32[18,128,128]{2,1,0:T(8,128)S(1)}, u32[]{:S(2)}) copy-start(f32[18,128,128]{2,1,0:T(8,128)S(1)} %get-tuple-element.33) | copy-start | bytes 3538948
  591.6 21.6 %all-to-all-start.13 = ((f32[16,128,128]{2,1,0:T(8,128)}), f32[16,128,128]{2,1,0:T(8,128)S(1)}, u32[]{:S(2)}, u32[]{:S(2)}) async-start(f32[16,128,128]{2,1,0:T(8,128)} %gather_fusion.16), calls=%async_computation.13 | async-start | bytes 2097152 | tf_op jit(solution)/shard_map/all_to_all | solution.py:73
  613.1 53.8 %all-to-all-start.12 = ((f32[32,128,128]{2,1,0:T(8,128)}), f32[32,128,128]{2,1,0:T(8,128)}, u32[]{:S(2)}, u32[]{:S(2)}) async-start(f32[32,128,128]{2,1,0:T(8,128)} %gather_fusion.15), calls=%async_computation.12 | async-start | bytes 4194304 | tf_op jit(solution)/shard_map/all_to_all | solution.py:72
  618.6 308.4 %all-reduce.3.cloned.1.call-start = ((), (), s32[]{:S(2)}) async-start(), calls=%async_computation.14 | async-start | bytes 262144 | tf_op jit(solution)/shard_map/psum | solution.py:106
Sparse Core Ops, SparseCore 0:
  688.2 238.6 all-reduce.2
where the time goes:
time: 971 us; the launch traced here: 961 us
  waiting for transfers between devices  415 us (43%)
  blocking collectives  296 us (30%)
  matrix products  64 us (7%)
  starting transfers between devices  61.4 us (6%)
  local copies, waits for them, and re-layouts  58.6 us (6%)
  other arithmetic  51.2 us (5%)
  between operations  14.4 us (1%)
    psum x1, waiting for transfers between devices, body(): gram, projected = lax.psum((basis_part, ritz_part), ('dom', 'dev'))  239 us
    all_to_all x4, blocking collectives, apply_laplacian(): lax.all_to_all(scaled[serve_inner], 'dev', split_axis=0, concat_axis=0, t...  216 us
    all_to_all x2, waiting for transfers between devices, apply_laplacian(): lax.all_to_all(scaled[serve_inner], 'dev', split_axis=0, concat_axis=0, t...  93.4 us
    psum x1, blocking collectives, body(): totals = lax.psum(squares, ('dom', 'dev'))  80 us
    all_to_all x6, waiting for transfers between devices, apply_laplacian(): lax.all_to_all(scaled[serve_outer], 'dom', split_axis=0, concat_axis=0, t...  77.4 us
    dot_general x6, matrix products, apply_laplacian(): jnp.einsum('rkij,rkjw->riw', weights_float, operand, precision=lax.Precis...  57.2 us
    all_to_all x6, starting transfers between devices, apply_laplacian(): lax.all_to_all(scaled[serve_outer], 'dom', split_axis=0, concat_axis=0, t...  38.9 us
    gather x6, local copies, waits for them, and re-layouts, apply_laplacian(): operand = sources[source_index]  31.5 us
  transfers between devices with their start and end apart: 11, of which 10 were waited for; matrix products, arithmetic and copies ran while one was open for 3% of the time, Pallas kernels for 0%

commit v1 on v0

v1 whole, which is shorter than its diff:
```python
import functools

import jax
import jax.numpy as jnp
from jax import lax
from jax.experimental import pallas as pl
from jax.experimental.pallas import tpu as pltpu
from jax.sharding import PartitionSpec as P

TILE = 128
WIDTH = 128
TROWS = 18
DEGREE = 5
N_DOM = 8
N_DEV = 32
NROWS = 589824
HALF = 64
INNER = (1, 2, 3, 4, -1, -2, -3, -4, 16)
OUTER = ((0, 1), (1, 0), (1, 1), (2, 0), (2, 1), (3, 0), (3, 1))
N_IN = 9
N_OUT = 7
N_MSG = N_IN + N_OUT
N_SLOT = N_MSG + 4
N_SRC = TROWS + N_SLOT

epsilon = 1e-06
center = 1.025
half_width = 0.975

MESH = pl.DeviceIdType.MESH
NT = (((1,), (1,)), ((), ()))


def tables(columns):
    dom = lax.axis_index("dom")
    dev = lax.axis_index("dev")
    flat = columns.reshape(-1)
    owner = flat // TROWS
    tile = flat % TROWS
    part = owner // N_DEV
    is_local = owner == dom * N_DEV + dev
    is_outer = part != dom
    is_inner = jnp.logical_not(is_local | is_outer)
    off = (owner % N_DEV - dev) % N_DEV
    inner_slot = jnp.where(off <= 4, off - 1, jnp.where(off == 16, 8, 35 - off))
    dy = (part // 2 - dom // 2) % 4
    dc = (part + dom) % 2
    outer_slot = 2 * dy + dc - 1
    ids = jnp.arange(flat.shape[0], dtype=jnp.int32)
    same = is_outer[None, :] & is_outer[:, None] & (part[None, :] == part[:, None]) & (ids[None, :] < ids[:, None])
    is_extra = jnp.any(same, axis=1)
    source = jnp.where(
        is_local,
        tile,
        jnp.where(
            is_inner,
            TROWS + inner_slot,
            jnp.where(is_extra, TROWS + N_MSG + dy, TROWS + N_IN + outer_slot),
        ),
    )
    slot = jnp.where(is_inner, inner_slot, jnp.where(is_outer & jnp.logical_not(is_extra), N_IN + outer_slot, -1))
    msg_ids = jnp.arange(N_MSG, dtype=jnp.int32)[:, None]
    base = jnp.sum(jnp.where(slot[None, :] == msg_ids, tile[None, :], 0), axis=1)
    out_ids = msg_ids - N_IN
    relayed = (out_ids > 0) & (out_ids % 2 == 1) & (outer_slot[None, :] == out_ids + 1)
    extra = jnp.where(
        is_extra[None, :],
        jnp.where(
            outer_slot[None, :] == out_ids,
            tile[None, :],
            jnp.where(relayed, TROWS + (out_ids + 1) // 2 - 1, 0),
        ),
        0,
    )
    extra = jnp.sum(extra, axis=1)
    lanes = jnp.arange(128, dtype=jnp.int32)[None, :]
    msg = jnp.where(lanes == 0, base[:, None], jnp.where(lanes == 1, extra[:, None], 0))
    return source.astype(jnp.int32), msg.astype(jnp.int32)[:, None, :]


def split(x):
    hi = x.astype(jnp.bfloat16)
    mid = (x - hi.astype(jnp.float32)).astype(jnp.bfloat16)
    return hi, mid


def quad(x):
    n = x.shape[0] // 2
    return (x[n:, 128:] + x[n:, :128]) + (x[:n, 128:] + x[:n, :128])


def kernel(
    source, msg, start, weights,
    filtered, ritz,
    wb, scale, y, zf, zb, part, mul, stage, recv, relay,
    got, serve, fb, ib, sq, sqs, sqd, sqx, sqz, red, r1, r2, r3, rg, mat_a, mat_m,
    msg_ss, msg_rs, smem_sem, ss, rs, relay_ss, relay_rs,
    sq_ss, sq_rs, g_ss, g_rs,
):
    dom = lax.axis_index("dom")
    dev = lax.axis_index("dev")
    yy, core = dom // 2, dom % 2
    zz, xx = dev // 4, dev % 4

    def inner_peer(offset):
        return (dom, (dev + offset + N_DEV) % N_DEV)

    def outer_peer(dy, dc):
        return (((yy + dy) % 4) * 2 + (core + dc) % 2, dev)

    def x_peer(d):
        return (dom, zz * 4 + (xx + d) % 4)

    def z_peer(d):
        return (dom, ((zz + d) % 8) * 4 + xx)

    def requester(s):
        if s < N_IN:
            return inner_peer(-INNER[s])
        dy, dc = OUTER[s - N_IN]
        return outer_peer(4 - dy, dc)

    barrier = pltpu.get_barrier_semaphore()
    peers = [inner_peer(o) for o in INNER] + [outer_peer(*o) for o in OUTER]
    peers += [z_peer(d) for d in (2, 3, 5, 6)]
    for peer in peers:
        pl.semaphore_signal(barrier, inc=1, device_id=peer, device_id_type=MESH)

    def turn(r, total):
        tile = start[r].T
        y[0, 0, r] = tile[:HALF]
        y[0, 1, r] = tile[HALF:]
        y[1, 0, r] = jnp.zeros((HALF, TILE), jnp.float32)
        y[1, 1, r] = jnp.zeros((HALF, TILE), jnp.float32)
        return total + tile * tile

    squares = lax.fori_loop(0, TROWS, turn, jnp.zeros((WIDTH, TILE), jnp.float32))
    mul[...] = jnp.ones_like(mul)
    sq[...] = lax.dot_general(
        jnp.ones((8, TILE), jnp.float32), squares, NT,
        precision=lax.Precision.HIGHEST, preferred_element_type=jnp.float32,
    )

    pl.semaphore_wait(barrier, len(peers))

    def msg_copy(s):
        return pltpu.make_async_remote_copy(
            src_ref=msg.at[s], dst_ref=got.at[s], send_sem=msg_ss.at[s], recv_sem=msg_rs.at[s],
            device_id=inner_peer(INNER[s]) if s < N_IN else outer_peer(*OUTER[s - N_IN]),
            device_id_type=MESH,
        )

    for s in range(N_MSG):
        msg_copy(s).start()

    def dom_copy(src, dst, o, send, recv_sem):
        dy, dc = OUTER[o]
        return pltpu.make_async_remote_copy(
            src_ref=src, dst_ref=dst, send_sem=send, recv_sem=recv_sem,
            device_id=outer_peer(dy, dc), device_id_type=MESH,
        )

    def sq_dom(o):
        return dom_copy(sq, sqd.at[o], o, sq_ss.at[o], sq_rs.at[o])

    def sq_x(d):
        return pltpu.make_async_remote_copy(
            src_ref=sqs.at[0], dst_ref=sqx.at[d - 1], send_sem=sq_ss.at[6 + d], recv_sem=sq_rs.at[6 + d],
            device_id=x_peer(d), device_id_type=MESH,
        )

    def sq_z(d):
        return pltpu.make_async_remote_copy(
            src_ref=sqs.at[1], dst_ref=sqz.at[d - 1], send_sem=sq_ss.at[9 + d], recv_sem=sq_rs.at[9 + d],
            device_id=z_peer(d), device_id_type=MESH,
        )

    for o in range(N_OUT):
        sq_dom(o).start()

    ones = jnp.ones((8, 256), jnp.bfloat16)

    def prepare(r, _):
        degree = jnp.zeros((8, 256), jnp.float32)
        for k in range(4):
            w = weights[r, k].astype(jnp.float32)
            hi, lo = split(w)
            cols = pl.ds((k % 2) * 128, 128)
            wb[r, k // 2, pl.ds(0, 128), cols] = hi
            wb[r, k // 2, pl.ds(128, 128), cols] = lo
        for p in range(2):
            degree += lax.dot_general(ones, wb[r, p], NT, preferred_element_type=jnp.float32)
        scale[r] = lax.rsqrt(degree[:, :128] + degree[:, 128:])
        return 0

    lax.fori_loop(0, TROWS, prepare, 0)

    for s in range(N_MSG):
        msg_copy(s).wait()
    to_smem = pltpu.make_async_copy(got, serve, smem_sem)
    to_smem.start()
    to_smem.wait()

    def put_scaled(h, r, value):
        z = value * scale[r, pl.ds(0, 1), :]
        zf[h, r] = z
        hi, mid = split(z)
        zb[h, r, pl.ds(0, HALF), :] = hi
        zb[h, r, pl.ds(HALF, HALF), :] = mid

    def slot_copy(h, par, s):
        if s < N_MSG:
            to = requester(s)
        elif s == N_MSG:
            to = outer_peer(0, 1)
        else:
            to = outer_peer(4 - (s - N_MSG), 0)
        return pltpu.make_async_remote_copy(
            src_ref=stage.at[h, s], dst_ref=recv.at[h, par, s],
            send_sem=ss.at[h, s], recv_sem=rs.at[h, par, s],
            device_id=to, device_id_type=MESH,
        )

    def relay_copy(h, par, d):
        return pltpu.make_async_remote_copy(
            src_ref=stage.at[h, N_SLOT + d], dst_ref=relay.at[h, par, d],
            send_sem=relay_ss.at[h, d], recv_sem=relay_rs.at[h, par, d],
            device_id=outer_peer(0, 1), device_id_type=MESH,
        )

    def send_first(h, par):
        for d in range(3):
            stage[h, N_SLOT + d] = zf[h, serve[N_IN + 2 * (d + 1), 0, 1]]
            relay_copy(h, par, d).start()
        for s in (9, 10, 11, 12, 13, 14, 15, 8, 7, 3, 6, 2, 5, 1, 4, 0, 16):
            index = serve[N_IN, 0, 1] if s == N_MSG else serve[s, 0, 0]
            stage[h, s] = zf[h, index]
            slot_copy(h, par, s).start()

    def send_last(h, par):
        for d in range(3):
            relay_copy(h, par, d).wait_recv()
            zf[h, TROWS + d] = relay[h, par, d]
        for d in range(3):
            s = N_MSG + 1 + d
            stage[h, s] = zf[h, serve[N_IN + 2 * (d + 1) - 1, 0, 1]]
            slot_copy(h, par, s).start()

    def operand(h, r, k):
        return jnp.concatenate([zb[h, source[4 * r + k]], zb[h, source[4 * r + k + 1]]], axis=1)

    def near(h):
        def one(r, _):
            part[h, r] = quad(lax.dot_general(operand(h, r, 0), wb[r, 0], NT, preferred_element_type=jnp.float32))
            return 0
        lax.fori_loop(0, TROWS, one, 0, unroll=6)

    for h in range(2):
        def first(r, _):
            put_scaled(h, r, y[0, h, r])
            return 0
        lax.fori_loop(0, TROWS, first, 0)
        send_first(h, 0)
    for h in range(2):
        near(h)
        send_last(h, 0)

    def iteration(it, _):
        s, h = it // 2, it % 2
        par = s % 2

        @pl.when(it == 2)
        def _():
            for o in range(N_OUT):
                sq_dom(o).wait()
            total = sq[...]
            for o in range(N_OUT):
                total += sqd[o]
            sqs[0] = total
            for d in range(1, 4):
                sq_x(d).start()

        @pl.when(it == 4)
        def _():
            for d in range(1, 4):
                sq_x(d).wait()
            sqs[1] = (sqs[0] + sqx[0]) + (sqx[1] + sqx[2])
            for d in range(1, 8):
                sq_z(d).start()

        @pl.when(it == 8)
        def _():
            for d in range(1, 8):
                sq_z(d).wait()
            total = sqs[1]
            for d in range(7):
                total += sqz[d]
            factor = lax.rsqrt(total[:1] / NROWS + epsilon)
            factor = jnp.broadcast_to(factor, (WIDTH, WIDTH)).T
            mul[0] = factor[:HALF]
            mul[1] = factor[HALF:]

        @pl.when(it == 10)
        def _():
            mul[...] = jnp.ones_like(mul)

        for q in range(N_SLOT):
            slot_copy(h, par, q).wait_recv()

        def widen(q, _):
            hi, mid = split(recv[h, par, q])
            zb[h, TROWS + q, pl.ds(0, HALF), :] = hi
            zb[h, TROWS + q, pl.ds(HALF, HALF), :] = mid
            return 0
        lax.fori_loop(0, N_SLOT, widen, 0, unroll=4)

        def far(r, _):
            part[h, r] += quad(lax.dot_general(operand(h, r, 2), wb[r, 1], NT, preferred_element_type=jnp.float32))
            return 0
        lax.fori_loop(0, TROWS, far, 0, unroll=6)

        last = s == DEGREE
        a = jnp.where(s == 0, (1 - center) / half_width, jnp.where(last, 1.0, 2 * (1 - center) / half_width)).astype(jnp.float32)
        b = jnp.where(s == 0, -1 / half_width, jnp.where(last, -1.0, -2 / half_width)).astype(jnp.float32)
        c = jnp.where((s == 0) | last, 0.0, -1.0).astype(jnp.float32)

        def update(r, _):
            value = a * y[par, h, r] + b * (part[h, r] * scale[r, pl.ds(0, 1), :]) + c * y[1 - par, h, r]
            value = value * mul[h]
            y[1 - par, h, r] = value
            put_scaled(h, r, value)
            return 0
        lax.fori_loop(0, TROWS, update, 0, unroll=3)

        for q in range(N_SLOT):
            slot_copy(h, par, q).wait_send()
        for d in range(3):
            relay_copy(h, par, d).wait_send()

        @pl.when(s < DEGREE)
        def _():
            send_first(h, 1 - par)
            near(h)
            send_last(h, 1 - par)
        return 0

    lax.fori_loop(0, 2 * (DEGREE + 1), iteration, 0)

    def finish(r, _):
        value = jnp.concatenate([y[1, 0, r], y[1, 1, r]], axis=0)
        filtered[r] = value.T
        hi, mid = split(value)
        fb[r, pl.ds(0, 128), :] = hi
        fb[r, pl.ds(128, 128), :] = mid
        hi, mid = split(jnp.concatenate([y[0, 0, r], y[0, 1, r]], axis=0))
        ib[r, pl.ds(0, 128), :] = hi
        ib[r, pl.ds(128, 128), :] = mid
        return 0
    lax.fori_loop(0, TROWS, finish, 0)

    def gram(r, carry):
        left = fb[r]
        return (
            carry[0] + lax.dot_general(left, left, NT, preferred_element_type=jnp.float32),
            carry[1] + lax.dot_general(left, ib[r], NT, preferred_element_type=jnp.float32),
        )
    zero = jnp.zeros((256, 256), jnp.float32)
    sums = lax.fori_loop(0, TROWS, gram, (zero, zero))
    for i in range(2):
        block = quad(sums[i])
        for d in range(N_DOM):
            red[d, pl.ds(16 * i, 16), :] = block[16 * d:16 * d + 16]

    def g1(o):
        dy, dc = OUTER[o]
        peer_dom = ((yy + dy) % 4) * 2 + (core + dc) % 2
        return dom_copy(red.at[peer_dom], r1.at[o], o, g_ss.at[o], g_rs.at[o])

    for o in range(N_OUT):
        g1(o).start()
    for o in range(N_OUT):
        g1(o).wait()
    total = red[dom]
    for o in range(N_OUT):
        total += r1[o]
    r2[xx] = total

    def g2(d, src):
        return pltpu.make_async_remote_copy(
            src_ref=r2.at[xx], dst_ref=r2.at[src], send_sem=g_ss.at[6 + d], recv_sem=g_rs.at[7 + src],
            device_id=x_peer(d), device_id_type=MESH,
        )

    for d in range(1, 4):
        g2(d, xx).start()
    for d in range(1, 4):
        g2(d, xx).wait_send()
        g2(d, (xx + d) % 4).wait_recv()
    r3[zz] = (r2[0] + r2[1]) + (r2[2] + r2[3])

    def g3(d, src):
        return pltpu.make_async_remote_copy(
            src_ref=r3.at[zz], dst_ref=r3.at[src], send_sem=g_ss.at[9 + d], recv_sem=g_rs.at[11 + src],
            device_id=z_peer(d), device_id_type=MESH,
        )

    for d in range(1, 8):
        g3(d, zz).start()
    for d in range(1, 8):
        g3(d, zz).wait_send()
        g3(d, (zz + d) % 8).wait_recv()
    total = r3[0]
    for d in range(1, 8):
        total += r3[d]
    rg[dom] = total * (1.0 / NROWS)

    def g4(o, src):
        dy, dc = OUTER[o]
        return dom_copy(rg.at[dom], rg.at[src], o, g_ss.at[17 + o], g_rs.at[19 + src])

    for o in range(N_OUT):
        g4(o, dom).start()
    for o in range(N_OUT):
        dy, dc = OUTER[o]
        g4(o, dom).wait_send()
        g4(o, ((yy + dy) % 4) * 2 + (core + dc) % 2).wait_recv()

    rows = lax.broadcasted_iota(jnp.int32, (WIDTH, WIDTH), 0)
    cols = lax.broadcasted_iota(jnp.int32, (WIDTH, WIDTH), 1)
    mat_a[...] = jnp.concatenate([rg[d, pl.ds(0, 16), :] for d in range(N_DOM)], axis=0)
    mat_m[...] = jnp.where(rows == cols, 1.0, 0.0)
    projected = jnp.concatenate([rg[d, pl.ds(16, 16), :] for d in range(N_DOM)], axis=0)

    def eliminate(j, _):
        a = mat_a[...]
        row_a = mat_a[pl.ds(j, 1), :]
        row_m = mat_m[pl.ds(j, 1), :]
        column = jnp.sum(jnp.where(cols == j, a, 0.0), axis=1, keepdims=True)
        pivot = jnp.sum(jnp.where(cols[:1] == j, row_a, 0.0), axis=1, keepdims=True)
        multiplier = jnp.where(rows[:, :1] > j, column / pivot, 0.0)
        mat_a[...] = a - multiplier * row_a
        mat_m[...] = mat_m[...] - multiplier * row_m
        return 0
    lax.fori_loop(0, WIDTH, eliminate, 0)
    pivots = jnp.sum(jnp.where(rows == cols, mat_a[...], 0.0), axis=1, keepdims=True)
    inverse = mat_m[...] * lax.rsqrt(pivots)
    left = jnp.dot(inverse, projected, precision=lax.Precision.HIGHEST, preferred_element_type=jnp.float32)
    ritz[...] = lax.dot_general(left, inverse, NT, precision=lax.Precision.HIGHEST, preferred_element_type=jnp.float32)


def body(start_block, columns, edge_weights):
    source, msg = tables(columns)
    f32, bf16 = jnp.float32, jnp.bfloat16
    vmem = pl.BlockSpec(memory_space=pltpu.VMEM)
    dma = pltpu.SemaphoreType.DMA
    filtered, ritz = pl.pallas_call(
        kernel,
        out_shape=(
            jax.ShapeDtypeStruct((TROWS, TILE, WIDTH), f32),
            jax.ShapeDtypeStruct((WIDTH, WIDTH), f32),
        ),
        in_specs=[pl.BlockSpec(memory_space=pltpu.SMEM), vmem, vmem, vmem],
        out_specs=(vmem, vmem),
        scratch_shapes=[
            pltpu.VMEM((TROWS, 2, 256, 256), bf16),
            pltpu.VMEM((TROWS, 8, TILE), f32),
            pltpu.VMEM((2, 2, TROWS, HALF, TILE), f32),
            pltpu.VMEM((2, TROWS + 3, HALF, TILE), f32),
            pltpu.VMEM((2, N_SRC, 2 * HALF, TILE), bf16),
            pltpu.VMEM((2, TROWS, HALF, TILE), f32),
            pltpu.VMEM((2, HALF, TILE), f32),
            pltpu.VMEM((2, N_SLOT + 3, HALF, TILE), f32),
            pltpu.VMEM((2, 2, N_SLOT, HALF, TILE), f32),
            pltpu.VMEM((2, 2, 3, HALF, TILE), f32),
            pltpu.VMEM((N_MSG, 1, 128), jnp.int32),
            pltpu.SMEM((N_MSG, 1, 128), jnp.int32),
            pltpu.VMEM((TROWS, 256, TILE), bf16),
            pltpu.VMEM((TROWS, 256, TILE), bf16),
            pltpu.VMEM((8, 128), f32),
            pltpu.VMEM((2, 8, 128), f32),
            pltpu.VMEM((7, 8, 128), f32),
            pltpu.VMEM((3, 8, 128), f32),
            pltpu.VMEM((7, 8, 128), f32),
            pltpu.VMEM((N_DOM, 32, 128), f32),
            pltpu.VMEM((7, 32, 128), f32),
            pltpu.VMEM((4, 32, 128), f32),
            pltpu.VMEM((8, 32, 128), f32),
            pltpu.VMEM((N_DOM, 32, 128), f32),
            pltpu.VMEM((WIDTH, WIDTH), f32),
            pltpu.VMEM((WIDTH, WIDTH), f32),
            dma((N_MSG,)), dma((N_MSG,)), dma,
            dma((2, N_SLOT)), dma((2, 2, N_SLOT)), dma((2, 3)), dma((2, 2, 3)),
            dma((17,)), dma((17,)), dma((24,)), dma((27,)),
        ],
        compiler_params=pltpu.CompilerParams(
            collective_id=0, has_side_effects=True, vmem_limit_bytes=56 * 2**20
        ),
        cost_estimate=pl.CostEstimate(flops=8_000_000_000, bytes_accessed=8_000_000, transcendentals=0),
    )(source, msg, start_block.reshape(TROWS, TILE, WIDTH), edge_weights)
    return filtered.reshape(TROWS * TILE, WIDTH), ritz


def solution(mesh):
    in_specs = (
        P(("dom", "dev"), None),
        P(("dom", "dev"), None),
        P(("dom", "dev"), None, None, None),
    )
    out_specs = (P(("dom", "dev"), None), P())
    return jax.shard_map(body, mesh=mesh, in_specs=in_specs, out_specs=out_specs, check_vma=False)
```

time: 971 us -> 125 us (0.13); the launches traced: 961 us -> 125 us
  waiting for transfers between devices: 415 us -> 0 us
  blocking collectives: 296 us -> 0 us
  Pallas kernels: 0 us -> 117 us
  matrix products: 64 us -> 0 us
  starting transfers between devices: 61.4 us -> 0 us
  local copies, waits for them, and re-layouts: 58.6 us -> 3.61 us
  other arithmetic: 51.2 us -> 3.06 us
  between operations: 14.4 us -> 0.7 us
    psum x1 -> x0, waiting for transfers between devices: 239 us -> none  [body(): gram, projected = lax.psum((basis_part, ritz_part), ('dom', 'dev'))]
    all_to_all x4 -> x0, blocking collectives: 216 us -> none  [apply_laplacian(): lax.all_to_all(scaled[serve_inner], 'dev', split_axis=0, concat_axis=0, t...]
    all_to_all x10 -> x0, waiting for transfers between devices: 176 us -> none  [the longest x2 93.4 us: apply_laplacian(): lax.all_to_all(scaled[serve_inner], 'dev', split_axis=0, concat_axis=0, t...]
    pallas_call x0 -> x1, Pallas kernels: none -> 117 us  [body(): pl.pallas_call(kernel, out_shape=(jax.ShapeDtypeStruct((TROWS, TILE, WIDT...]
    psum x1 -> x0, blocking collectives: 80 us -> none  [body(): totals = lax.psum(squares, ('dom', 'dev'))]
    dot_general x8 -> x0, matrix products: 62.6 us -> none  [the longest x6 57.2 us: apply_laplacian(): jnp.einsum('rkij,rkjw->riw', weights_float, operand, precision=lax.Precis...]
    all_to_all x10 -> x0, starting transfers between devices: 60.9 us -> none  [the longest x6 38.9 us: apply_laplacian(): lax.all_to_all(scaled[serve_outer], 'dom', split_axis=0, concat_axis=0, t...]
    gather x18 -> x0, local copies, waits for them, and re-layouts: 54.3 us -> none  [the longest x6 31.5 us: apply_laplacian(): operand = sources[source_index]]
  transfers between devices with their start and end apart: 11 -> 0, of which waited for: 10 -> 0; matrix products, arithmetic and copies ran while one was open for 3% -> 0% of each run, Pallas kernels for 0% -> 0%
where the time goes in v1:
time: 125 us
  Pallas kernels  117 us (94%)
  local copies, waits for them, and re-layouts  3.61 us (3%)
  other arithmetic  3.06 us (2%)
    pallas_call x1, Pallas kernels, body(): pl.pallas_call(kernel, out_shape=(jax.ShapeDtypeStruct((TROWS, TILE, WIDT...  117 us
    unnamed x4, local copies, waits for them, and re-layouts  3.02 us

profile of v1, /device:TPU:1, one launch (start us, length us, event | category | flops | bytes accessed | tf_op | source)
XLA Modules:
  0.0 124.8 jit_solution(16463926421849344763)
XLA Ops:
  0.6 0.7 sign_compare_fusion
  1.4 0.1 copy.11
  1.5 0.1 ne.271
  1.6 0.7 broadcast_remainder_fusion
  2.3 0.1 copy.12
  2.4 0.1 rem.182
  2.5 0.1 copy.13
  2.6 0.1 div.66
  2.7 0.2 fusion.1
  2.9 0.5 and_select_fusion.9
  3.4 0.2 select_reduce_fusion
  3.6 0.7 broadcast_select_fusion.1.msg
  4.3 117.4 %shard_map.50 = (f32[18,128,128]{2,1,0:T(8,128)}, f32[128,128]{1,0:T(8,128)}) custom-call(s32[72]{0:T(128)} %get-tuple-element.18.source, s32[16,1,128]{2,1,0:T(1,128)} %broadcast_select_fusion.1.msg, f32[18,128,128]{2,1,0:T(8,128)} %bitcast.3, s32[18,4,128,128]{3,2,1,0:T(8,128)} %weights.1), custom_call_target="tpu_custom_call" | custom-call | flops 8000000000 | bytes 8000000 | tf_op jit(solution)/shard_map/pallas_call | solution.py:456
  121.7 0.0 copy-start
  121.8 2.4 %copy.16 = f32[2304,128]{1,0:T(8,128)} copy(f32[2304,128]{1,0:T(8,128)} %bitcast.2) | data formatting | bytes 2359296
  124.1 0.0 copy-done
  124.1 0.6 copy.17
  (6 shorter events, 0.1 us)
Async XLA Ops:
  121.7 2.4 %copy-start = (f32[128,128]{1,0:T(8,128)S(1)}, f32[128,128]{1,0:T(8,128)}, u32[]{:S(2)}) copy-start(f32[128,128]{1,0:T(8,128)} %get-tuple-element.27) | copy-start | bytes 196612

commit v2 on v1

v2 whole, which is shorter than its diff:
```python
import functools

import jax
import jax.numpy as jnp
from jax import lax
from jax.experimental import pallas as pl
from jax.experimental.pallas import tpu as pltpu
from jax.sharding import PartitionSpec as P

TILE = 128
WIDTH = 128
TROWS = 18
DEGREE = 5
N_DOM = 8
N_DEV = 32
NROWS = 589824
HALF = 64
INNER = (1, 2, 3, 4, -1, -2, -3, -4, 16)
OUTER = ((0, 1), (1, 0), (1, 1), (2, 0), (2, 1), (3, 0), (3, 1))
N_IN = 9
N_OUT = 7
N_MSG = N_IN + N_OUT
N_SLOT = N_MSG + 4
N_SRC = TROWS + N_SLOT

epsilon = 1e-06
center = 1.025
half_width = 0.975

MESH = pl.DeviceIdType.MESH
NT = (((1,), (1,)), ((), ()))


def split(x):
    hi = x.astype(jnp.bfloat16)
    mid = (x - hi.astype(jnp.float32)).astype(jnp.bfloat16)
    return hi, mid


def quad(x):
    n = x.shape[0] // 2
    return (x[n:, 128:] + x[n:, :128]) + (x[:n, 128:] + x[:n, :128])


def kernel(
    columns, start_hbm, weights_hbm,
    filtered, ritz,
    source, src_v, msg, start, weights, turned,
    wb, scale, y, zf, zb, part, mul, stage, recv, relay,
    got, serve, fb, ib, sq, sqs, sqd, sqx, sqz, red, r1, r2, r3, rg, mat_a, mat_m, lin,
    in_sem, out_sem, msg_ss, msg_rs, smem_sem, ss, rs, relay_ss, relay_rs,
    sq_ss, sq_rs, g_ss, g_rs,
):
    dom = lax.axis_index("dom")
    dev = lax.axis_index("dev")
    yy, core = dom >> 1, dom & 1
    zz, xx = dev >> 2, dev & 3

    inner = {o: (dom, (dev + o) & (N_DEV - 1)) for o in INNER}
    inner.update({-16: inner[16]})
    outer_doms = {
        (dy, dc): (((yy + dy) & 3) << 1) + ((core + dc) & 1) for dy in range(4) for dc in range(2)
    }
    outer = {key: (value, dev) for key, value in outer_doms.items()}
    x_places = {d: (xx + d) & 3 for d in range(1, 4)}
    z_places = {d: (zz + d) & 7 for d in range(1, 8)}
    x_peers = {d: (dom, (zz << 2) + x_places[d]) for d in range(1, 4)}
    z_peers = {d: (dom, (z_places[d] << 2) + xx) for d in range(1, 8)}

    def inner_peer(offset):
        return inner[offset]

    def outer_peer(dy, dc):
        return outer[dy & 3, dc]

    def x_peer(d):
        return x_peers[d]

    def z_peer(d):
        return z_peers[d]

    def requester(s):
        if s < N_IN:
            return inner_peer(-INNER[s])
        dy, dc = OUTER[s - N_IN]
        return outer_peer(4 - dy, dc)

    barrier = pltpu.get_barrier_semaphore()
    peers = [inner_peer(o) for o in INNER] + [outer_peer(*o) for o in OUTER]
    peers += [z_peer(d) for d in (2, 3, 5, 6)]
    for peer in peers:
        pl.semaphore_signal(barrier, inc=1, device_id=peer, device_id_type=MESH)

    start_copy = pltpu.make_async_copy(start_hbm, start, in_sem.at[0])
    start_copy.start()

    def weights_copy(p):
        return pltpu.make_async_copy(
            weights_hbm.at[pl.ds(6 * p, 6)], weights.at[pl.ds(6 * p, 6)], in_sem.at[1 + p]
        )

    for p in range(3):
        weights_copy(p).start()

    listed = columns[...]
    owner = (listed * 3641) >> 16
    tile = listed - owner * TROWS
    owner_part = owner >> 5
    is_local = owner == dom * N_DEV + dev
    is_outer = owner_part != dom
    off = ((owner & (N_DEV - 1)) - dev) & (N_DEV - 1)
    inner_slot = jnp.where(off <= 4, off - 1, jnp.minimum(35 - off, 8))
    dy = ((owner_part >> 1) - yy) & 3
    outer_slot = 2 * dy + ((owner_part + dom) & 1) - 1
    slot = jnp.where(is_outer, N_IN + outer_slot, jnp.where(is_local, -1, inner_slot))
    order = lax.broadcasted_iota(jnp.int32, (TROWS, 4), 0) * 4 + lax.broadcasted_iota(jnp.int32, (TROWS, 4), 1)
    code = order * 32 + tile
    lanes = lax.broadcasted_iota(jnp.int32, (1, 128), 1)
    is_extra = jnp.zeros((TROWS, 4), jnp.bool_)
    bases, extras, doubled = [], [], []
    for s in range(N_MSG):
        mask = slot == s
        lowest = jnp.min(jnp.min(jnp.where(mask, code, 1 << 20), axis=0, keepdims=True), axis=1, keepdims=True)
        bases.append(lowest & 31)
        if s >= N_IN:
            highest = jnp.max(jnp.max(jnp.where(mask, code, -1), axis=0, keepdims=True), axis=1, keepdims=True)
            is_extra = is_extra | (mask & (code == highest) & (code > lowest))
            doubled.append(highest > lowest)
            extras.append(jnp.where(highest > lowest, highest & 31, 0))
    for s in range(N_MSG):
        row = jnp.where(lanes == 0, bases[s], 0)
        if s >= N_IN:
            o = s - N_IN
            extra = extras[o]
            if o % 2 == 1:
                extra = jnp.where(doubled[o + 1], TROWS + (o + 1) // 2 - 1, extra)
            row = jnp.where(lanes == 1, extra, row)
        msg[s] = row
    src_v[...] = jnp.zeros_like(src_v)
    src_v[pl.ds(0, TROWS), pl.ds(0, 4)] = jnp.where(
        is_outer,
        jnp.where(is_extra, TROWS + N_MSG + dy, TROWS + N_IN + outer_slot),
        jnp.where(is_local, tile, TROWS + inner_slot),
    )
    source_copy = pltpu.make_async_copy(src_v, source, in_sem.at[4])
    source_copy.start()

    pl.semaphore_wait(barrier, len(peers))

    def msg_copy(s):
        return pltpu.make_async_remote_copy(
            src_ref=msg.at[s], dst_ref=got.at[s], send_sem=msg_ss.at[s], recv_sem=msg_rs.at[s],
            device_id=inner_peer(INNER[s]) if s < N_IN else outer_peer(*OUTER[s - N_IN]),
            device_id_type=MESH,
        )

    for s in range(N_MSG):
        msg_copy(s).start()

    start_copy.wait()

    def turn(r, total):
        value = start[r].T
        y[0, 0, r] = value[:HALF]
        y[0, 1, r] = value[HALF:]
        y[1, 0, r] = jnp.zeros((HALF, TILE), jnp.float32)
        y[1, 1, r] = jnp.zeros((HALF, TILE), jnp.float32)
        return total + value * value

    squares = lax.fori_loop(0, TROWS, turn, jnp.zeros((WIDTH, TILE), jnp.float32), unroll=3)
    mul[...] = jnp.ones_like(mul)
    sq[...] = lax.dot_general(
        jnp.ones((8, TILE), jnp.float32), squares, NT,
        precision=lax.Precision.HIGHEST, preferred_element_type=jnp.float32,
    )

    def dom_copy(src, dst, o, send, recv_sem):
        dy, dc = OUTER[o]
        return pltpu.make_async_remote_copy(
            src_ref=src, dst_ref=dst, send_sem=send, recv_sem=recv_sem,
            device_id=outer_peer(dy, dc), device_id_type=MESH,
        )

    def sq_dom(o):
        return dom_copy(sq, sqd.at[o], o, sq_ss.at[o], sq_rs.at[o])

    def sq_x(d):
        return pltpu.make_async_remote_copy(
            src_ref=sqs.at[0], dst_ref=sqx.at[d - 1], send_sem=sq_ss.at[6 + d], recv_sem=sq_rs.at[6 + d],
            device_id=x_peer(d), device_id_type=MESH,
        )

    def sq_z(d):
        return pltpu.make_async_remote_copy(
            src_ref=sqs.at[1], dst_ref=sqz.at[d - 1], send_sem=sq_ss.at[9 + d], recv_sem=sq_rs.at[9 + d],
            device_id=z_peer(d), device_id_type=MESH,
        )

    for o in range(N_OUT):
        sq_dom(o).start()

    ones = jnp.ones((8, TILE), jnp.bfloat16)

    def degrees(r, _):
        total = (weights[r, 0] + weights[r, 1]) + (weights[r, 2] + weights[r, 3])
        hi, lo = split(total.astype(jnp.float32))
        degree = lax.dot_general(ones, hi, NT, preferred_element_type=jnp.float32)
        degree += lax.dot_general(ones, lo, NT, preferred_element_type=jnp.float32)
        scale[r] = lax.rsqrt(degree)
        return 0

    for p in range(3):
        weights_copy(p).wait()
        lax.fori_loop(6 * p, 6 * p + 6, degrees, 0, unroll=6)

    def prepare(r, _):
        for k in range(4):
            hi, lo = split(weights[r, k].astype(jnp.float32).T)
            place = pl.ds((k % 2) * 128, 128)
            wb[r, k // 2, place, pl.ds(0, 128)] = hi
            wb[r, k // 2, place, pl.ds(128, 128)] = lo
        return 0

    def put_scaled(h, r, value):
        z = value * scale[r, pl.ds(0, 1), :]
        zf[h, r] = z
        hi, mid = split(z)
        zb[h, r, pl.ds(0, HALF), :] = hi
        zb[h, r, pl.ds(HALF, HALF), :] = mid

    def slot_copy(h, par, s):
        if s < N_MSG:
            to = requester(s)
        elif s == N_MSG:
            to = outer_peer(0, 1)
        else:
            to = outer_peer(4 - (s - N_MSG), 0)
        return pltpu.make_async_remote_copy(
            src_ref=stage.at[h, s], dst_ref=recv.at[h, par, s],
            send_sem=ss.at[h, s], recv_sem=rs.at[h, par, s],
            device_id=to, device_id_type=MESH,
        )

    def relay_copy(h, par, d):
        return pltpu.make_async_remote_copy(
            src_ref=stage.at[h, N_SLOT + d], dst_ref=relay.at[h, par, d],
            send_sem=relay_ss.at[h, d], recv_sem=relay_rs.at[h, par, d],
            device_id=outer_peer(0, 1), device_id_type=MESH,
        )

    def send_first(h, par):
        for d in range(3):
            stage[h, N_SLOT + d] = zf[h, serve[N_IN + 2 * (d + 1), 0, 1]]
            relay_copy(h, par, d).start()
        for s in (9, 10, 11, 12, 13, 14, 15, 8, 7, 3, 6, 2, 5, 1, 4, 0, 16):
            index = serve[N_IN, 0, 1] if s == N_MSG else serve[s, 0, 0]
            stage[h, s] = zf[h, index]
            slot_copy(h, par, s).start()

    def send_last(h, par):
        for d in range(3):
            relay_copy(h, par, d).wait_recv()
            zf[h, TROWS + d] = relay[h, par, d]
        for d in range(3):
            s = N_MSG + 1 + d
            stage[h, s] = zf[h, serve[N_IN + 2 * (d + 1) - 1, 0, 1]]
            slot_copy(h, par, s).start()

    def operand(h, r, k):
        return jnp.concatenate([zb[h, source[r, k]], zb[h, source[r, k + 1]]], axis=1)

    def near(h):
        def one(r, _):
            part[h, r] = quad(jnp.dot(operand(h, r, 0), wb[r, 0], preferred_element_type=jnp.float32))
            return 0
        lax.fori_loop(0, TROWS, one, 0, unroll=18)

    for h in range(2):
        def first(r, _):
            put_scaled(h, r, y[0, h, r])
            return 0
        lax.fori_loop(0, TROWS, first, 0, unroll=3)
    for s in range(N_MSG):
        msg_copy(s).wait()
    to_smem = pltpu.make_async_copy(got, serve, smem_sem)
    to_smem.start()
    to_smem.wait()
    source_copy.wait()
    for h in range(2):
        send_first(h, 0)
    for h in range(2):
        send_last(h, 0)
    lax.fori_loop(0, TROWS, prepare, 0, unroll=3)
    for h in range(2):
        near(h)

    def outer_dom(o):
        return outer_doms[OUTER[o]]

    def g1(m, o):
        return dom_copy(red.at[m, outer_dom(o)], r1.at[m, o], o, g_ss.at[m, o], g_rs.at[m, o])

    def g2(m, d, src):
        return pltpu.make_async_remote_copy(
            src_ref=r2.at[m, xx], dst_ref=r2.at[m, src], send_sem=g_ss.at[m, 6 + d], recv_sem=g_rs.at[m, 7 + src],
            device_id=x_peer(d), device_id_type=MESH,
        )

    def g3(m, d, src):
        return pltpu.make_async_remote_copy(
            src_ref=r3.at[m, zz], dst_ref=r3.at[m, src], send_sem=g_ss.at[m, 9 + d], recv_sem=g_rs.at[m, 11 + src],
            device_id=z_peer(d), device_id_type=MESH,
        )

    def g4(m, o, src):
        return dom_copy(rg.at[m, dom], rg.at[m, src], o, g_ss.at[m, 17 + o], g_rs.at[m, 19 + src])

    def sum_start(m, block):
        for d in range(N_DOM):
            red[m, d] = block[16 * d:16 * d + 16]
        for o in range(N_OUT):
            g1(m, o).start()

    def sum_x(m):
        for o in range(N_OUT):
            g1(m, o).wait()
        total = red[m, dom]
        for o in range(N_OUT):
            total += r1[m, o]
        r2[m, xx] = total
        for d in range(1, 4):
            g2(m, d, xx).start()

    def sum_z(m):
        for d in range(1, 4):
            g2(m, d, xx).wait_send()
            g2(m, d, x_places[d]).wait_recv()
        r3[m, zz] = (r2[m, 0] + r2[m, 1]) + (r2[m, 2] + r2[m, 3])
        for d in range(1, 8):
            g3(m, d, zz).start()

    def sum_back(m):
        for d in range(1, 8):
            g3(m, d, zz).wait_send()
            g3(m, d, z_places[d]).wait_recv()
        total = r3[m, 0]
        for d in range(1, 8):
            total += r3[m, d]
        rg[m, dom] = total * (1.0 / NROWS)
        for o in range(N_OUT):
            g4(m, o, dom).start()

    def sum_end(m):
        for o in range(N_OUT):
            g4(m, o, dom).wait_send()
            g4(m, o, outer_dom(o)).wait_recv()
        return jnp.concatenate([rg[m, d] for d in range(N_DOM)], axis=0)

    def widen_block(dst, par):
        def one(r, _):
            lane = pl.ds(pl.multiple_of(r * TILE, TILE), TILE)
            for h in range(2):
                hi, mid = split(y[par, h, r])
                dst[pl.ds(HALF * h, HALF), lane] = hi
                dst[pl.ds(WIDTH + HALF * h, HALF), lane] = mid
            return 0
        lax.fori_loop(0, TROWS, one, 0, unroll=3)

    def iteration(it, _):
        s, h = it >> 1, it & 1
        par = s & 1

        @pl.when(it == 2)
        def _():
            for o in range(N_OUT):
                sq_dom(o).wait()
            total = sq[...]
            for o in range(N_OUT):
                total += sqd[o]
            sqs[0] = total
            for d in range(1, 4):
                sq_x(d).start()

        @pl.when(it == 4)
        def _():
            for d in range(1, 4):
                sq_x(d).wait()
            sqs[1] = (sqs[0] + sqx[0]) + (sqx[1] + sqx[2])
            for d in range(1, 8):
                sq_z(d).start()

        @pl.when(it == 8)
        def _():
            for d in range(1, 8):
                sq_z(d).wait()
            total = sqs[1]
            for d in range(7):
                total += sqz[d]
            factor = lax.rsqrt(total[:1] / NROWS + epsilon)
            factor = jnp.broadcast_to(factor, (WIDTH, WIDTH)).T
            mul[0] = factor[:HALF]
            mul[1] = factor[HALF:]

        @pl.when(it == 10)
        def _():
            mul[...] = jnp.ones_like(mul)
            widen_block(fb, 1)
            sum_start(0, quad(lax.dot_general(fb[...], fb[...], NT, preferred_element_type=jnp.float32)))

        @pl.when(it == 11)
        def _():
            sum_x(0)

        for q in range(N_SLOT):
            slot_copy(h, par, q).wait_recv()

        def widen(q, _):
            hi, mid = split(recv[h, par, q])
            zb[h, TROWS + q, pl.ds(0, HALF), :] = hi
            zb[h, TROWS + q, pl.ds(HALF, HALF), :] = mid
            return 0
        lax.fori_loop(0, N_SLOT, widen, 0, unroll=4)

        def far(r, _):
            part[h, r] += quad(jnp.dot(operand(h, r, 2), wb[r, 1], preferred_element_type=jnp.float32))
            return 0
        lax.fori_loop(0, TROWS, far, 0, unroll=18)

        last = s == DEGREE
        a = jnp.where(s == 0, (1 - center) / half_width, jnp.where(last, 1.0, 2 * (1 - center) / half_width)).astype(jnp.float32)
        b = jnp.where(s == 0, -1 / half_width, jnp.where(last, -1.0, -2 / half_width)).astype(jnp.float32)
        c = jnp.where((s == 0) | last, 0.0, -1.0).astype(jnp.float32)

        def update(r, _):
            value = a * y[par, h, r] + b * (part[h, r] * scale[r, pl.ds(0, 1), :]) + c * y[1 - par, h, r]
            value = value * mul[h]
            y[1 - par, h, r] = value
            put_scaled(h, r, value)
            return 0
        lax.fori_loop(0, TROWS, update, 0, unroll=6)

        for q in range(N_SLOT):
            slot_copy(h, par, q).wait_send()
        for d in range(3):
            relay_copy(h, par, d).wait_send()

        @pl.when(s < DEGREE)
        def _():
            send_first(h, 1 - par)
            near(h)
            send_last(h, 1 - par)
        return 0

    lax.fori_loop(0, 2 * (DEGREE + 1), iteration, 0)

    widen_block(ib, 0)
    sum_start(1, quad(lax.dot_general(fb[...], ib[...], NT, preferred_element_type=jnp.float32)))
    sum_z(0)

    def finish(r, _):
        turned[r] = jnp.concatenate([y[1, 0, r], y[1, 1, r]], axis=0).T
        return 0
    lax.fori_loop(0, TROWS, finish, 0, unroll=3)
    out_copy = pltpu.make_async_copy(turned, filtered, out_sem)
    out_copy.start()

    sum_x(1)
    sum_back(0)
    sum_z(1)
    rows = lax.broadcasted_iota(jnp.int32, (WIDTH, WIDTH), 0)
    cols = lax.broadcasted_iota(jnp.int32, (WIDTH, WIDTH), 1)
    mat_a[...] = sum_end(0)
    mat_m[...] = jnp.where(rows == cols, 1.0, 0.0)

    def eliminate(block, _):
        a = mat_a[...]
        m = mat_m[...]
        done = []
        for i in (0, 2, 4, 6):
            a0, a1, m0, m1 = a[i:i + 1], a[i + 1:i + 2], m[i:i + 1], m[i + 1:i + 2]
            p00, p01, p11 = a0[:, i:i + 1], a0[:, i + 1:i + 2], a1[:, i + 1:i + 2]
            q = 1.0 / p00
            low = p01 * q
            schur = p11 - p01 * low
            t = 1.0 / schur
            u1 = t * (a1 - low * a0)
            u0 = q * a0 - low * u1
            n1 = m1 - low * m0
            v1 = t * n1
            v0 = q * m0 - low * v1
            done += [lax.rsqrt(p00) * m0, lax.rsqrt(schur) * n1]
            keep = rows[:, :1] > i + 1
            c0 = jnp.where(keep, a[:, i:i + 1], 0.0)
            c1 = jnp.where(keep, a[:, i + 1:i + 2], 0.0)
            a = a - c0 * u0 - c1 * u1
            m = m - c0 * v0 - c1 * v1
        lin[pl.ds(pl.multiple_of(block * 8, 8), 8), :] = jnp.concatenate(done, axis=0)
        a = pltpu.roll(a, WIDTH - 8, 1)
        mat_a[pl.ds(0, 120), :] = a[8:]
        mat_a[pl.ds(120, 8), :] = a[:8]
        mat_m[pl.ds(0, 120), :] = m[8:]
        mat_m[pl.ds(120, 8), :] = m[:8]
        return 0

    lax.fori_loop(0, 8, eliminate, 0)
    sum_back(1)
    lax.fori_loop(8, 16, eliminate, 0)
    projected = sum_end(1)
    inverse = lin[...]
    left = jnp.dot(inverse, projected, precision=lax.Precision.HIGHEST, preferred_element_type=jnp.float32)
    ritz[...] = lax.dot_general(left, inverse, NT, precision=lax.Precision.HIGHEST, preferred_element_type=jnp.float32)
    out_copy.wait()


def body(start_block, columns, edge_weights):
    f32, bf16 = jnp.float32, jnp.bfloat16
    vmem = pl.BlockSpec(memory_space=pltpu.VMEM)
    hbm = pl.BlockSpec(memory_space=pl.ANY)
    dma = pltpu.SemaphoreType.DMA
    filtered, ritz = pl.pallas_call(
        kernel,
        out_shape=(
            jax.ShapeDtypeStruct((TROWS, TILE, WIDTH), f32),
            jax.ShapeDtypeStruct((WIDTH, WIDTH), f32),
        ),
        in_specs=[vmem, hbm, hbm],
        out_specs=(hbm, vmem),
        scratch_shapes=[
            pltpu.SMEM((24, 128), jnp.int32),
            pltpu.VMEM((24, 128), jnp.int32),
            pltpu.VMEM((N_MSG, 1, 128), jnp.int32),
            pltpu.VMEM((TROWS, TILE, WIDTH), f32),
            pltpu.VMEM((TROWS, 4, TILE, TILE), jnp.int32),
            pltpu.VMEM((TROWS, TILE, WIDTH), f32),
            pltpu.VMEM((TROWS, 2, 256, 256), bf16),
            pltpu.VMEM((TROWS, 8, TILE), f32),
            pltpu.VMEM((2, 2, TROWS, HALF, TILE), f32),
            pltpu.VMEM((2, TROWS + 3, HALF, TILE), f32),
            pltpu.VMEM((2, N_SRC, 2 * HALF, TILE), bf16),
            pltpu.VMEM((2, TROWS, HALF, TILE), f32),
            pltpu.VMEM((2, HALF, TILE), f32),
            pltpu.VMEM((2, N_SLOT + 3, HALF, TILE), f32),
            pltpu.VMEM((2, 2, N_SLOT, HALF, TILE), f32),
            pltpu.VMEM((2, 2, 3, HALF, TILE), f32),
            pltpu.VMEM((N_MSG, 1, 128), jnp.int32),
            pltpu.SMEM((N_MSG, 1, 128), jnp.int32),
            pltpu.VMEM((256, TROWS * TILE), bf16),
            pltpu.VMEM((256, TROWS * TILE), bf16),
            pltpu.VMEM((8, 128), f32),
            pltpu.VMEM((2, 8, 128), f32),
            pltpu.VMEM((7, 8, 128), f32),
            pltpu.VMEM((3, 8, 128), f32),
            pltpu.VMEM((7, 8, 128), f32),
            pltpu.VMEM((2, N_DOM, 16, 128), f32),
            pltpu.VMEM((2, 7, 16, 128), f32),
            pltpu.VMEM((2, 4, 16, 128), f32),
            pltpu.VMEM((2, 8, 16, 128), f32),
            pltpu.VMEM((2, N_DOM, 16, 128), f32),
            pltpu.VMEM((WIDTH, WIDTH), f32),
            pltpu.VMEM((WIDTH, WIDTH), f32),
            pltpu.VMEM((WIDTH, WIDTH), f32),
            dma((5,)), dma, dma((N_MSG,)), dma((N_MSG,)), dma,
            dma((2, N_SLOT)), dma((2, 2, N_SLOT)), dma((2, 3)), dma((2, 2, 3)),
            dma((17,)), dma((17,)), dma((2, 24)), dma((2, 27)),
        ],
        compiler_params=pltpu.CompilerParams(
            collective_id=0, has_side_effects=True, vmem_limit_bytes=56 * 2**20
        ),
        cost_estimate=pl.CostEstimate(flops=8_000_000_000, bytes_accessed=8_000_000, transcendentals=0),
    )(columns, start_block.reshape(TROWS, TILE, WIDTH), edge_weights)
    return filtered.reshape(TROWS * TILE, WIDTH), ritz


def solution(mesh):
    in_specs = (
        P(("dom", "dev"), None),
        P(("dom", "dev"), None),
        P(("dom", "dev"), None, None, None),
    )
    out_specs = (P(("dom", "dev"), None), P())
    return jax.shard_map(body, mesh=mesh, in_specs=in_specs, out_specs=out_specs, check_vma=False)
```

time: 125 us -> 105 us (0.84)
  Pallas kernels: 117 us -> 99.4 us
  other arithmetic: 3.06 us -> 0 us
    pallas_call x1, Pallas kernels: 117 us -> 99.4 us  [body(): pl.pallas_call(kernel, out_shape=(jax.ShapeDtypeStruct((TROWS, TILE, WIDT...]
    unnamed x4 -> x5, local copies, waits for them, and re-layouts: 3.02 us -> 4.39 us
    select_n x3 -> x0, other arithmetic: 1.26 us -> none  [the longest x1 0.71 us: tables(): jnp.where(lanes == 0, base[:, None], jnp.where(lanes == 1, extra[:, None]...]
where the time goes in v2:
time: 105 us; the launch traced here: 104 us
  Pallas kernels  99.4 us (95%)
  local copies, waits for them, and re-layouts  4.39 us (4%)
    pallas_call x1, Pallas kernels, body(): pl.pallas_call(kernel, out_shape=(jax.ShapeDtypeStruct((TROWS, TILE, WIDT...  99.4 us
    unnamed x5, local copies, waits for them, and re-layouts  4.39 us

profile of v2, /device:TPU:1, one launch (start us, length us, event | category | flops | bytes accessed | tf_op | source)
XLA Modules:
  0.0 104.4 jit_solution(18381531996029928253)
XLA Ops:
  0.6 1.4 %copy.5.columns = s32[18,4]{1,0:T(8,128)} copy(s32[18,4]{0,1:T(4,128)} %param.4) | data formatting | bytes 576 | tf_op args[1]
  2.0 99.4 %shard_map.50 = (f32[18,128,128]{2,1,0:T(8,128)}, f32[128,128]{1,0:T(8,128)}) custom-call(s32[18,4]{1,0:T(8,128)} %copy.5.columns, f32[18,128,128]{2,1,0:T(8,128)} %bitcast.3, s32[18,4,128,128]{3,2,1,0:T(8,128)} %weights_hbm.1), custom_call_target="tpu_custom_call" | custom-call | flops 8000000000 | bytes 8000000 | tf_op jit(solution)/shard_map/pallas_call | solution.py:520
  101.4 0.0 copy-start
  101.4 2.4 %copy.8 = f32[2304,128]{1,0:T(8,128)} copy(f32[2304,128]{1,0:T(8,128)} %bitcast.2) | data formatting | bytes 2359296
  103.8 0.0 copy-done
  103.8 0.6 copy.9
Async XLA Ops:
  101.4 2.4 %copy-start = (f32[128,128]{1,0:T(8,128)S(1)}, f32[128,128]{1,0:T(8,128)}, u32[]{:S(2)}) copy-start(f32[128,128]{1,0:T(8,128)} %get-tuple-element.9) | copy-start | bytes 196612

commit v3 on v2

--- a/solution.py
+++ b/solution.py
@@ -22,6 +22,7 @@
 N_MSG = N_IN + N_OUT
 N_SLOT = N_MSG + 4
 N_SRC = TROWS + N_SLOT
+STEPS = 1
 
 epsilon = 1e-06
 center = 1.025
@@ -113,10 +114,10 @@
     dy = ((owner_part >> 1) - yy) & 3
     outer_slot = 2 * dy + ((owner_part + dom) & 1) - 1
     slot = jnp.where(is_outer, N_IN + outer_slot, jnp.where(is_local, -1, inner_slot))
-    order = lax.broadcasted_iota(jnp.int32, (TROWS, 4), 0) * 4 + lax.broadcasted_iota(jnp.int32, (TROWS, 4), 1)
+    order = lax.broadcasted_iota(jnp.int32, (4, TROWS), 0) * TROWS + lax.broadcasted_iota(jnp.int32, (4, TROWS), 1)
     code = order * 32 + tile
     lanes = lax.broadcasted_iota(jnp.int32, (1, 128), 1)
-    is_extra = jnp.zeros((TROWS, 4), jnp.bool_)
+    is_extra = jnp.zeros((4, TROWS), jnp.bool_)
     bases, extras, doubled = [], [], []
     for s in range(N_MSG):
         mask = slot == s
@@ -137,7 +138,7 @@
             row = jnp.where(lanes == 1, extra, row)
         msg[s] = row
     src_v[...] = jnp.zeros_like(src_v)
-    src_v[pl.ds(0, TROWS), pl.ds(0, 4)] = jnp.where(
+    src_v[pl.ds(0, 4), pl.ds(0, TROWS)] = jnp.where(
         is_outer,
         jnp.where(is_extra, TROWS + N_MSG + dy, TROWS + N_IN + outer_slot),
         jnp.where(is_local, tile, TROWS + inner_slot),
@@ -267,7 +268,7 @@
             slot_copy(h, par, s).start()
 
     def operand(h, r, k):
-        return jnp.concatenate([zb[h, source[r, k]], zb[h, source[r, k + 1]]], axis=1)
+        return jnp.concatenate([zb[h, source[k, r]], zb[h, source[k + 1, r]]], axis=1)
 
     def near(h):
         def one(r, _):
@@ -526,8 +527,8 @@
         in_specs=[vmem, hbm, hbm],
         out_specs=(hbm, vmem),
         scratch_shapes=[
-            pltpu.SMEM((24, 128), jnp.int32),
-            pltpu.VMEM((24, 128), jnp.int32),
+            pltpu.SMEM((8, 128), jnp.int32),
+            pltpu.VMEM((8, 128), jnp.int32),
             pltpu.VMEM((N_MSG, 1, 128), jnp.int32),
             pltpu.VMEM((TROWS, TILE, WIDTH), f32),
             pltpu.VMEM((TROWS, 4, TILE, TILE), jnp.int32),
@@ -567,8 +568,25 @@
             collective_id=0, has_side_effects=True, vmem_limit_bytes=56 * 2**20
         ),
         cost_estimate=pl.CostEstimate(flops=8_000_000_000, bytes_accessed=8_000_000, transcendentals=0),
-    )(columns, start_block.reshape(TROWS, TILE, WIDTH), edge_weights)
-    return filtered.reshape(TROWS * TILE, WIDTH), ritz
+    )(columns.T, start_block.reshape(TROWS, TILE, WIDTH), edge_weights)
+    def write(block, small, out_block, out_small):
+        out_block[...] = block[...]
+
+        @pl.when(pl.program_id(0) == 0)
+        def _():
+            out_small[...] = small[...]
+
+    rows = TROWS * TILE // STEPS
+    return tuple(pl.pallas_call(
+        write,
+        grid=(STEPS,),
+        out_shape=(
+            jax.ShapeDtypeStruct((TROWS * TILE, WIDTH), f32),
+            jax.ShapeDtypeStruct((WIDTH, WIDTH), f32),
+        ),
+        in_specs=[pl.BlockSpec((rows, WIDTH), lambda i: (i, 0)), pl.BlockSpec((WIDTH, WIDTH), lambda i: (0, 0))],
+        out_specs=(pl.BlockSpec((rows, WIDTH), lambda i: (i, 0)), pl.BlockSpec((WIDTH, WIDTH), lambda i: (0, 0))),
+    )(filtered.reshape(TROWS * TILE, WIDTH), ritz))
 
 
 def solution(mesh):

time: 105 us -> 103 us (0.981)
  local copies, waits for them, and re-layouts: 4.39 us -> 0 us
  Pallas kernels: 99.4 us -> 102 us
    unnamed x5 -> x0, local copies, waits for them, and re-layouts: 4.39 us -> none
    pallas_call x0 -> x1, Pallas kernels: none -> 2.37 us  [body(): pl.pallas_call(write, grid=(STEPS,), out_shape=(jax.ShapeDtypeStruct((TRO...]
where the time goes in v3:
time: 103 us
  Pallas kernels  102 us (99%)
    pallas_call x1, Pallas kernels, body(): pl.pallas_call(kernel, out_shape=(jax.ShapeDtypeStruct((TROWS, TILE, WIDT...  99.5 us
    pallas_call x1, Pallas kernels, body(): pl.pallas_call(write, grid=(STEPS,), out_shape=(jax.ShapeDtypeStruct((TRO...  2.37 us

profile of v3, /device:TPU:1, one launch (start us, length us, event | category | flops | bytes accessed | tf_op | source)
XLA Modules:
  0.0 102.5 jit_solution(14493153537042584226)
XLA Ops:
  0.6 99.5 %shard_map.50 = (f32[18,128,128]{2,1,0:T(8,128)}, f32[128,128]{1,0:T(8,128)}) custom-call(s32[4,18]{1,0:T(4,128)} %bitcast.5, f32[18,128,128]{2,1,0:T(8,128)} %bitcast.4, s32[18,4,128,128]{3,2,1,0:T(8,128)} %weights_hbm.1), custom_call_target="tpu_custom_call" | custom-call | flops 8000000000 | bytes 8000000 | tf_op jit(solution)/shard_map/pallas_call | solution.py:521
  100.2 2.4 %shard_map.51 = (f32[2304,128]{1,0:T(8,128)}, f32[128,128]{1,0:T(8,128)}) custom-call(f32[2304,128]{1,0:T(8,128)} %bitcast.3, f32[128,128]{1,0:T(8,128)} %get-tuple-element.5.small), custom_call_target="tpu_custom_call" | custom-call | tf_op jit(solution)/shard_map/pallas_call | solution.py:580
